TPU v7x, 256 devices: a whole 4x4x8 slice. The times are simulated.
256 devices in a mesh: probe: 8 (over y, x_hi), tm: 16 (over x_lo, z), lane: 2 (over core).
Axes of the slice: x: 4 (x_hi: 2, x_lo: 2; x = x_hi * 2 + x_lo), y: 4, z: 8, core: 2. Of those that a mesh axis runs over, the one named last changes fastest.
Arguments:
- volt: bfloat16 [8, 2, 4096, 480], P('probe', 'lane', 'tm'), may hold values from -40 to 40
- keep: int32 [8, 2, 4096], P('probe', 'lane', 'tm'), may hold values 0 or 1
- site_ids: int32 [8, 2], P('probe', 'lane'), may hold values from 0 to 59
- probe_ids: int32 [8], P('probe'), may hold values from 0 to 7, each once
- w_patch: bfloat16 [480, 768], replicated, may hold values from -0.25 to 0.25
- site_table: bfloat16 [60, 768], replicated, may hold values from -3 to 3
- probe_table: bfloat16 [8, 768], replicated, may hold values from -3 to 3
- mask_token: bfloat16 [768], replicated, may hold values from -3 to 3
- gain_time: bfloat16 [768], replicated, may hold values from 0.099609375 to 1.8984375
- w_qkv_time: bfloat16 [768, 2304], replicated, may hold values from -6 to 6
- w_out_time: bfloat16 [768, 768], replicated, may hold values from -0.21875 to 0.21875
- gain_cross: bfloat16 [768], replicated, may hold values from 0.099609375 to 1.8984375
- w_qkv_cross: bfloat16 [768, 2304], replicated, may hold values from -6 to 6
- w_out_cross: bfloat16 [768, 768], replicated, may hold values from -0.21875 to 0.21875
Outputs:
- encoded: bfloat16 [8, 2, 4096, 768], P('probe', 'lane', 'tm')
All inputs are finite; a program needn't handle non-finite values. No bound on the sum of `keep` on one device may be relied on, other than what follows from the above.
Results may differ from a plain program's by a relative error of at most 0.024.
Values may be sent and summed in bfloat16 or wider, within the bound.
No kernel may reach another device: no remote copies, remote signals or barrier semaphores. Data moves between devices by JAX's collectives and lax.ppermute only.
A program may use at most 192 MiB of HBM per device.

v0:
```python
import math
import jax
import jax.numpy as jnp
from jax import lax
from jax.sharding import PartitionSpec as P

HEADS = 12
HEAD_DIM = 64
WIN = 16


def time_code(times, width):
    half = width // 2
    freq = jnp.exp(jnp.arange(half, dtype=jnp.float32) * (-math.log(10000.0) / half))
    angle = times.astype(jnp.float32)[:, None] * freq[None, :]
    return jnp.concatenate([jnp.sin(angle), jnp.cos(angle)], axis=1)


def layer_norm(rows, gain):
    middle = jnp.mean(rows, axis=-1, keepdims=True)
    centred = rows - middle
    spread = jnp.mean(centred * centred, axis=-1, keepdims=True)
    return centred * lax.rsqrt(spread + 1e-05) * gain.astype(jnp.float32)


def lookup(ids, table):
    onehot = (ids[:, None] == jnp.arange(table.shape[0], dtype=jnp.int32)[None, :]).astype(
        table.dtype
    )
    found = jnp.dot(onehot, table, preferred_element_type=jnp.float32)
    return found


def body(
    volt,
    keep,
    site_ids,
    probe_ids,
    w_patch,
    site_table,
    probe_table,
    mask_token,
    gain_time,
    w_qkv_time,
    w_out_time,
    gain_cross,
    w_qkv_cross,
    w_out_cross,
):
    width = w_patch.shape[1]
    scale = 1.0 / math.sqrt(HEAD_DIM)
    volt_rows = volt[0]
    lanes = volt_rows.shape[0]
    tdev = volt_rows.shape[1]
    first = lax.axis_index("tm") * tdev
    site_vec = lookup(site_ids[0], site_table)
    probe_vec = lookup(probe_ids, probe_table)[0]
    mask_rows = keep[0].astype(jnp.bfloat16)
    kv_time = w_qkv_time[:, width:]
    filler = mask_token.astype(jnp.float32)
    count = volt_rows.shape[1]
    proj = jnp.einsum("stc,cd->std", volt_rows, w_patch, preferred_element_type=jnp.float32)
    proj = jnp.where((keep[0] == 1)[..., None], proj, filler[None, None, :])
    code = time_code(first + jnp.arange(count, dtype=jnp.int32), width)
    x0 = (proj + site_vec[:, None, :] + probe_vec[None, None, :] + code[None]).astype(jnp.bfloat16)
    h1 = layer_norm(x0.astype(jnp.float32), gain_time).astype(jnp.bfloat16)
    queries = jnp.einsum(
        "std,de->ste", h1, w_qkv_time[:, :width], preferred_element_type=jnp.float32
    ).astype(jnp.bfloat16)
    query_heads = queries.reshape(lanes, tdev, HEADS, HEAD_DIM)
    query_pos = first + jnp.arange(tdev, dtype=jnp.int32)
    start_top = jnp.full((lanes, HEADS, tdev), -1e30, jnp.float32)
    both = jnp.einsum("std,de->ste", h1, kv_time, preferred_element_type=jnp.float32).astype(
        jnp.bfloat16
    )
    own_keys = both[..., :width]
    own_values = both[..., width:]
    keys = lax.all_gather(own_keys, "tm", axis=1, tiled=True)
    top = start_top
    count = keys.shape[1]
    key_heads = keys.reshape(lanes, count, HEADS, HEAD_DIM)
    value_heads = lax.all_gather(own_values, "tm", axis=1, tiled=True).reshape(
        lanes, count, HEADS, HEAD_DIM
    )
    scores = (
        jnp.einsum("sqhc,skhc->shqk", query_heads, key_heads, preferred_element_type=jnp.float32)
        * scale
    )
    key_pos = jnp.arange(count, dtype=jnp.int32)
    allowed = (lax.all_gather(mask_rows, "tm", axis=1, tiled=True)[:, None, None, :] == 1) | (
        query_pos[None, None, :, None] == key_pos[None, None, None, :]
    )
    new_top = jnp.maximum(top, jnp.max(jnp.where(allowed, scores, -1e30), axis=-1))
    weights = jnp.where(allowed, jnp.exp(scores - new_top[..., None]), 0.0)
    total = jnp.sum(weights, axis=-1)
    acc = jnp.einsum(
        "shqk,skhc->shqc",
        weights.astype(jnp.bfloat16),
        value_heads,
        preferred_element_type=jnp.float32,
    )
    context = acc / total[..., None]
    ctx1 = jnp.transpose(context, (0, 2, 1, 3)).reshape(lanes, tdev, width).astype(jnp.bfloat16)
    x1 = (
        x0.astype(jnp.float32)
        + jnp.einsum("std,de->ste", ctx1, w_out_time, preferred_element_type=jnp.float32)
    ).astype(jnp.bfloat16)
    slab, slab_mask = (
        lax.all_to_all(x1[None], "probe", split_axis=2, concat_axis=0, tiled=True),
        lax.all_to_all(mask_rows[None], "probe", split_axis=2, concat_axis=0, tiled=True),
    )
    probes = slab.shape[0]
    slab_len = slab.shape[2]
    nwin = slab_len // WIN
    h2 = layer_norm(slab.astype(jnp.float32), gain_cross).astype(jnp.bfloat16)
    cross_queries = jnp.einsum(
        "pstd,de->pste", h2, w_qkv_cross[:, :width], preferred_element_type=jnp.float32
    ).astype(jnp.bfloat16)
    kv_cross = w_qkv_cross[:, width:]
    own_kv = jnp.einsum("pstd,de->pste", h2, kv_cross, preferred_element_type=jnp.float32).astype(
        jnp.bfloat16
    )
    all_kv, all_mask = (
        lax.all_gather(own_kv, "lane", axis=1, tiled=True),
        lax.all_gather(slab_mask, "lane", axis=1, tiled=True),
    )
    sites = all_kv.shape[1]
    query_win = cross_queries.reshape(probes, lanes, nwin, WIN, width).transpose(2, 0, 1, 3, 4)
    query_count = probes * lanes * WIN
    query_win = query_win.reshape(nwin, query_count, HEADS, HEAD_DIM)
    kv_win = all_kv.reshape(probes, sites, nwin, WIN, 2 * width).transpose(2, 0, 1, 3, 4)
    key_count = probes * sites * WIN
    kv_win = kv_win.reshape(nwin, key_count, 2 * width)
    key_heads = kv_win[..., :width].reshape(nwin, key_count, HEADS, HEAD_DIM)
    value_heads = kv_win[..., width:].reshape(nwin, key_count, HEADS, HEAD_DIM)
    mask_win = (
        all_mask.reshape(probes, sites, nwin, WIN).transpose(2, 0, 1, 3).reshape(nwin, key_count)
    )
    lane_first = lax.axis_index("lane") * lanes
    probe_part = jnp.arange(probes, dtype=jnp.int32)[:, None, None] * sites
    site_part = lane_first + jnp.arange(lanes, dtype=jnp.int32)[None, :, None]
    query_ids = (
        (probe_part + site_part) * WIN + jnp.arange(WIN, dtype=jnp.int32)[None, None, :]
    ).reshape(query_count)
    allowed = (mask_win[:, None, :] == 1) | (
        query_ids[None, :, None] == jnp.arange(key_count, dtype=jnp.int32)[None, None, :]
    )
    allowed = allowed[:, None, :, :]
    scores = (
        jnp.einsum("nqhc,nkhc->nhqk", query_win, key_heads, preferred_element_type=jnp.float32)
        * scale
    )
    top = jnp.max(jnp.where(allowed, scores, -1e30), axis=-1, keepdims=True)
    weights = jnp.where(allowed, jnp.exp(scores - top), 0.0)
    total = jnp.sum(weights, axis=-1)
    mixed = jnp.einsum(
        "nhqk,nkhc->nhqc",
        weights.astype(jnp.bfloat16),
        value_heads,
        preferred_element_type=jnp.float32,
    )
    context2 = mixed / total[..., None]
    ctx2 = jnp.transpose(context2, (0, 2, 1, 3)).reshape(nwin, probes, lanes, WIN, width)
    ctx2 = (
        ctx2.transpose(1, 2, 0, 3, 4).reshape(probes, lanes, slab_len, width).astype(jnp.bfloat16)
    )
    home = lax.all_to_all(ctx2, "probe", split_axis=0, concat_axis=2, tiled=True)
    out = x1.astype(jnp.float32) + jnp.einsum(
        "std,de->ste", home[0], w_out_cross, preferred_element_type=jnp.float32
    )
    return out.astype(jnp.bfloat16)[None]


def solution(mesh):
    return jax.shard_map(
        body,
        mesh=mesh,
        in_specs=(
            P("probe", "lane", "tm", None),
            P("probe", "lane", "tm"),
            P("probe", "lane"),
            P("probe"),
            P(),
            P(),
            P(),
            P(),
            P(),
            P(),
            P(),
            P(),
            P(),
            P(),
        ),
        out_specs=P("probe", "lane", "tm", None),
        check_vma=False,
    )
```

profile of v0, /device:TPU:1, one launch (start us, length us, event | category | flops | bytes accessed | tf_op | source)
XLA Modules:
  0.0 296.9 jit_solution(4322483236727782394)
XLA Ops:
  8.4 0.7 convert_element_type.146
  9.1 0.7 compare_reduce_fusion.1
  9.8 1.4 multiply_sine_fusion
  11.2 0.8 convolution_reduce_fusion
  12.0 1.0 convolution_reduce_fusion.1
  13.1 1.8 fusion.64
  15.1 0.8 fusion.11
  16.0 0.9 fusion.63
  17.0 0.7 all-gather.8.cloned.1.call-update
  17.7 1.8 convolution_convert_fusion.3
  19.7 32.5 %all-gather = bf16[1,1,4096]{2,1,0:T(2,128)(2,1)S(1)} all-gather(bf16[1,1,256]{2,1,0:T(2,128)(2,1)S(1)} %convert_element_type.150), channel_id=2, replica_groups=mesh['probe'=8,'tm'=16,'lane'=2] {'tm'}, dimensions={2}, use_global_device_ids=true | all-gather | bytes 8704 | tf_op jit(solution)/shard_map/all_gather | solution.py:90
  52.3 0.8 fusion.6
  53.1 46.5 %all-gather.6.cloned.1.call-done = bf16[1,4096,768]{2,1,0:T(8,128)(2,1)} async-done(((bf16[1,256,768]{2,1,0:T(8,128)(2,1)}), bf16[1,4096,768]{2,1,0:T(8,128)(2,1)}) %all-gather.6.cloned.1.call-update) | async-done | bytes 6291472 | tf_op jit(solution)/shard_map/all_gather | solution.py:78
  99.6 8.7 %copy.60 = bf16[1,4096,768]{1,2,0:T(8,128)(2,1)} copy(bf16[1,4096,768]{2,1,0:T(8,128)(2,1)} %all-gather.6.cloned.1.call-done) | data formatting | bytes 12582912 | tf_op jit(solution)/shard_map/all_gather | solution.py:78
  108.2 23.5 %select_reduce_fusion = (f32[12,256]{1,0:T(8,128)S(1)}, f32[12,256,4096]{2,1,0:T(8,128)}) fusion(pred[256,4096]{1,0:T(8,128)(4,1)S(1)} %fusion.6, bf16[256,12,64]{0,2,1:T(8,128)(2,1)S(1)} %bitcast.94, bf16[4096,12,64]{0,2,1:T(8,128)(2,1)} %bitcast.87), kind=kOutput, calls=%fused_computation.2 | convolution fusion | flops 1648358400 | bytes 58077184 | tf_op jit(solution)/shard_map/sqhc,skhc->shqk/dot_general | solution.py:86
  131.8 22.8 %fusion.1 = f32[12,256]{1,0:T(8,128)S(1)} fusion(f32[12,256,4096]{2,1,0:T(8,128)} %get-tuple-element.14, f32[12,256]{1,0:T(8,128)S(1)} %broadcast_maximum_fusion, pred[256,4096]{1,0:T(8,128)(4,1)S(1)} %fusion.6), kind=kLoop, calls=%fused_computation.3 | loop fusion | flops 50328576 | bytes 51404800 | tf_op jit(solution)/shard_map/reduce_sum | solution.py:95
  154.6 26.4 %all-gather.8.cloned.1.call-done = bf16[1,4096,768]{2,1,0:T(8,128)(2,1)} async-done(((bf16[1,256,768]{2,1,0:T(8,128)(2,1)}), bf16[1,4096,768]{2,1,0:T(8,128)(2,1)}) %all-gather.8.cloned.1.call-update) | async-done | bytes 6291472 | tf_op jit(solution)/shard_map/all_gather | solution.py:82
  181.0 8.7 %copy.61 = bf16[1,4096,768]{1,2,0:T(8,128)(2,1)} copy(bf16[1,4096,768]{2,1,0:T(8,128)(2,1)} %all-gather.8.cloned.1.call-done) | data formatting | bytes 12582912 | tf_op jit(solution)/shard_map/all_gather | solution.py:82
  189.7 21.7 %fusion.43 = bf16[12,256,64]{1,2,0:T(8,128)(2,1)} fusion(bf16[4096,12,64]{0,2,1:T(8,128)(2,1)} %bitcast.89, f32[12,256,4096]{2,1,0:T(8,128)} %get-tuple-element.14, f32[12,256]{1,0:T(8,128)S(1)} %broadcast_maximum_fusion, pred[256,4096]{1,0:T(8,128)(4,1)S(1)} %fusion.6, f32[12,256]{1,0:T(8,128)S(1)} %fusion.1), kind=kOutput, calls=%fused_computation.46 | convolution fusion | flops 1661337600 | bytes 58089472 | tf_op jit(solution)/shard_map/shqk,skhc->shqc/dot_general | solution.py:96
  211.4 1.5 fusion.31
  212.9 0.6 copy.79
  213.5 0.5 broadcast.245
  214.0 3.0 %reduce.23 = bf16[256,768]{1,0:T(8,128)(2,1)S(1)} reduce(bf16[256,1,1,768]{3,2,1,0:T(2,128)(2,1)S(1)} %bitcast.93, bf16[]{:T(256)} %broadcast.245), dimensions={1,2}, to_apply=%bitcast.84.reduce_sub_computation | reduce | bytes 786434
  217.1 0.8 reshape.439
  217.9 6.1 %all-to-all-start.1 = ((bf16[8,2,12288]{2,1,0:T(2,128)(2,1)}), bf16[8,2,12288]{2,1,0:T(2,128)(2,1)S(1)}, u32[]{:S(2)}, u32[]{:S(2)}) async-start(bf16[8,2,12288]{2,1,0:T(2,128)(2,1)} %reshape.439), calls=%async_computation.1 | async-start | bytes 786432 | tf_op jit(solution)/shard_map/all_to_all | solution.py:109
  224.0 8.3 %all-to-all-done.1 = bf16[8,2,12288]{2,1,0:T(2,128)(2,1)S(1)} async-done(((bf16[8,2,12288]{2,1,0:T(2,128)(2,1)}), bf16[8,2,12288]{2,1,0:T(2,128)(2,1)S(1)}, u32[]{:S(2)}, u32[]{:S(2)}) %all-to-all-start.1) | async-done | bytes 393248 | tf_op jit(solution)/shard_map/all_to_all | solution.py:109
  232.3 0.4 reshape.440
  232.7 1.2 convert_reduce_fusion
  233.9 3.6 %multiply_reduce_fusion = f32[256]{0:T(256)S(1)} fusion(f32[256]{0:T(256)S(1)} %broadcast_multiply_fusion, bf16[256,1,1,768]{3,2,1,0:T(2,128)(2,1)S(1)} %reshape.440), kind=kLoop, calls=%fused_computation.50 | loop fusion | flops 786176 | bytes 395264 | tf_op jit(solution)/shard_map/reduce_sum | solution.py:22
  237.6 3.4 %convolution_convert_fusion = bf16[8,32,1536]{2,1,0:T(8,128)(2,1)} fusion(bf16[768,2304]{1,0:T(8,128)(2,1)} %param.26, f32[8,32,768]{2,1,0:T(8,128)S(1)} %bitcast.100, f32[768]{0:T(1024)S(1)} %convert_element_type.167, f32[8,32]{1,0:T(8,128)S(1)} %rsqrt.21, f32[8,32]{1,0:T(8,128)S(1)} %div.39), kind=kOutput, calls=%fused_computation.13 | convolution fusion | flops 605159424 | bytes 3937280 | tf_op jit(solution)/shard_map/pstd,de->pste/dot_general | solution.py:120
  241.1 0.8 copy.62
  241.9 3.4 %all-to-all-start = ((bf16[1,1,256]{1,0,2:T(2,128)(2,1)}), bf16[1,1,256]{1,0,2:T(2,128)(2,1)S(1)}, u32[]{:S(2)}, u32[]{:S(2)}) async-start(bf16[1,1,256]{1,0,2:T(2,128)(2,1)} %copy.62), calls=%async_computation | async-start | bytes 262144 | tf_op jit(solution)/shard_map/all_to_all | solution.py:110
  245.5 6.7 %all-to-all-done = bf16[1,1,256]{1,0,2:T(2,128)(2,1)S(1)} async-done(((bf16[1,1,256]{1,0,2:T(2,128)(2,1)}), bf16[1,1,256]{1,0,2:T(2,128)(2,1)S(1)}, u32[]{:S(2)}, u32[]{:S(2)}) %all-to-all-start) | async-done | bytes 544 | tf_op jit(solution)/shard_map/all_to_all | solution.py:110
  252.3 1.0 reduce.18
  253.4 8.8 %all_gather.18 = bf16[8,2,32]{2,0,1:T(8,128)(2,1)S(1)} all-gather(bf16[8,1,32]{2,0,1:T(8,128)(2,1)S(1)} %all_to_all.9), channel_id=1, replica_groups=mesh['probe'=8,'tm'=16,'lane'=2] {'lane'}, dimensions={1}, use_global_device_ids=true | all-gather | bytes 1536 | tf_op jit(solution)/shard_map/all_gather | solution.py:125
  262.4 1.8 convolution_convert_fusion.2
  264.2 0.6 reshape.415
  264.9 1.5 copy.66
  266.4 1.3 fusion.62
  267.7 1.4 copy.67
  269.1 2.3 copy.69
  271.4 0.5 fusion.46
  271.9 1.4 fusion.65
  273.3 0.7 fusion.33
  274.0 0.8 copy.70
  274.8 0.6 convert_element_type.174
  275.5 12.4 %all_to_all.30 = bf16[8,1,32,768]{3,2,1,0:T(8,128)(2,1)S(1)} all-to-all(bf16[8,1,32,768]{3,2,1,0:T(8,128)(2,1)S(1)} %bitcast.97), channel_id=1, replica_groups=mesh['probe'=8,'tm'=16,'lane'=2] {'probe'}, dimensions={0} | all-to-all | bytes 786432 | tf_op jit(solution)/shard_map/all_to_all | solution.py:167
  287.9 2.5 fusion.36
  (47 shorter events, 1.5 us)
Async XLA Ops:
  6.5 204.9 %copy-start = (bf16[768,768]{1,0:T(8,128)(2,1)S(1)}, bf16[768,768]{1,0:T(8,128)(2,1)}, u32[]{:S(2)}) copy-start(bf16[768,768]{1,0:T(8,128)(2,1)} %param.24) | copy-start | bytes 3538948
  6.5 8.6 %copy-start.2 = (bf16[768]{0:T(1024)(128)(2,1)S(1)}, bf16[768]{0:T(1024)(128)(2,1)}, u32[]{:S(2)}) copy-start(bf16[768]{0:T(1024)(128)(2,1)} %param.22) | copy-start | bytes 4612
  6.5 93.0 %all-gather.6.cloned.1.call-start = ((), (), s32[]{:S(2)}) async-start(), calls=%async_computation.3 | async-start | bytes 6684672 | tf_op jit(solution)/shard_map/all_gather | solution.py:78
  6.6 8.6 %copy-start.5 = (bf16[768,2304]{1,0:T(8,128)(2,1)S(1)}, bf16[768,2304]{1,0:T(8,128)(2,1)}, u32[]{:S(2)}) copy-start(bf16[768,2304]{1,0:T(8,128)(2,1)} %param.23) | copy-start | bytes 10616836
  15.1 2.6 copy-start.4
  17.0 164.0 %all-gather.8.cloned.1.call-start = ((), (), s32[]{:S(2)}) async-start(), calls=%async_computation.4 | async-start | bytes 6684672 | tf_op jit(solution)/shard_map/all_gather | solution.py:82
  211.4 12.6 %copy-start.3 = (bf16[768]{0:T(1024)(128)(2,1)S(1)}, bf16[768]{0:T(1024)(128)(2,1)}, u32[]{:S(2)}) copy-start(bf16[768]{0:T(1024)(128)(2,1)} %param.25) | copy-start | bytes 4612
  217.9 14.4 %all-to-all-start.1 = ((bf16[8,2,12288]{2,1,0:T(2,128)(2,1)}), bf16[8,2,12288]{2,1,0:T(2,128)(2,1)S(1)}, u32[]{:S(2)}, u32[]{:S(2)}) async-start(bf16[8,2,12288]{2,1,0:T(2,128)(2,1)} %reshape.439), calls=%async_computation.1 | async-start | bytes 786432 | tf_op jit(solution)/shard_map/all_to_all | solution.py:109
  224.0 40.9 %all-gather.10.cloned.1.call-start = ((), (), s32[]{:S(2)}) async-start(), calls=%async_computation.5 | async-start | bytes 2359296 | tf_op jit(solution)/shard_map/all_gather | solution.py:124
  241.9 10.4 %all-to-all-start = ((bf16[1,1,256]{1,0,2:T(2,128)(2,1)}), bf16[1,1,256]{1,0,2:T(2,128)(2,1)S(1)}, u32[]{:S(2)}, u32[]{:S(2)}) async-start(bf16[1,1,256]{1,0,2:T(2,128)(2,1)} %copy.62), calls=%async_computation | async-start | bytes 262144 | tf_op jit(solution)/shard_map/all_to_all | solution.py:110
  271.9 1.4 copy-start.1
Sparse Core Ops, SparseCore 0:
  17.1 82.4 all-gather.5
  101.4 79.5 all-gather.7
  241.2 14.7 all-gather.9
where the time goes:
time: 298 us; the launch traced here: 297 us
  waiting for transfers between devices  88.6 us (30%)
  matrix products  62 us (21%)
  blocking collectives  53.7 us (18%)
  other arithmetic  37.1 us (12%)
  local copies, waits for them, and re-layouts  30.8 us (10%)
  between operations  15.2 us (5%)
  starting transfers between devices  9.53 us (3%)
    all_gather x1, waiting for transfers between devices, body(): keys = lax.all_gather(own_keys, 'tm', axis=1, tiled=True)  46.5 us
    all_gather x1, blocking collectives, body(): lax.all_gather(mask_rows, 'tm', axis=1, tiled=True)[:, None, None, :] == 1  32.5 us
    all_gather x1, waiting for transfers between devices, body(): lax.all_gather(own_values, 'tm', axis=1, tiled=True)  26.4 us
    dot_general x1, matrix products, body(): jnp.einsum('sqhc,skhc->shqk', query_heads, key_heads, preferred_element_t...  23.5 us
    reduce_sum x1, other arithmetic, body(): total = jnp.sum(weights, axis=-1)  22.8 us
    dot_general x1, matrix products, body(): jnp.einsum('shqk,skhc->shqc', weights.astype(jnp.bfloat16), value_heads,...  21.7 us
    all_to_all x1, blocking collectives, body(): lax.all_to_all(ctx2, 'probe', split_axis=0, concat_axis=2, tiled=True)  12.4 us
    all_gather x1, blocking collectives, body(): lax.all_gather(slab_mask, 'lane', axis=1, tiled=True)  8.77 us
  transfers between devices with their start and end apart: 5, of which 4 were waited for; matrix products, arithmetic and copies ran while one was open for 21% of the time, Pallas kernels for 0%

commit v1 on v0

--- a/solution.py
+++ b/solution.py
@@ -79,9 +79,9 @@
     top = start_top
     count = keys.shape[1]
     key_heads = keys.reshape(lanes, count, HEADS, HEAD_DIM)
-    value_heads = lax.all_gather(own_values, "tm", axis=1, tiled=True).reshape(
-        lanes, count, HEADS, HEAD_DIM
-    )
+    value_heads = jnp.concatenate(
+        lax.all_to_all(jnp.stack([own_values] * lax.axis_size("tm")), "tm", 0, 0), axis=1
+    ).reshape(lanes, count, HEADS, HEAD_DIM)
     scores = (
         jnp.einsum("sqhc,skhc->shqk", query_heads, key_heads, preferred_element_type=jnp.float32)
         * scale

time: 298 us -> 424 us (1.42)
  blocking collectives: 53.7 us -> 227 us
  waiting for transfers between devices: 88.6 us -> 15.1 us
  local copies, waits for them, and re-layouts: 30.8 us -> 44.7 us
  starting transfers between devices: 9.53 us -> 21.3 us
    all_gather x1, blocking collectives: 32.5 us -> 203 us  [body(): lax.all_gather(mask_rows, 'tm', axis=1, tiled=True)[:, None, None, :] == 1]
    all_gather x1, waiting for transfers between devices: 46.5 us -> 0.02 us  [body(): keys = lax.all_gather(own_keys, 'tm', axis=1, tiled=True)]
    all_gather x1 -> x0, waiting for transfers between devices: 26.4 us -> none  [body(): lax.all_gather(own_values, 'tm', axis=1, tiled=True)]
    another operation x0 -> x2, local copies, waits for them, and re-layouts: none -> 13.6 us
    all_to_all x0 -> x1, starting transfers between devices: none -> 10.2 us  [body(): lax.all_to_all(jnp.stack([own_values] * lax.axis_size('tm')), 'tm', 0, 0)]
    all_to_all x0 -> x1, local copies, waits for them, and re-layouts: none -> 8.95 us  [body(): lax.all_to_all(jnp.stack([own_values] * lax.axis_size('tm')), 'tm', 0, 0)]
    all_gather x1 -> x0, local copies, waits for them, and re-layouts: 8.67 us -> none  [body(): lax.all_gather(own_values, 'tm', axis=1, tiled=True)]
  transfers between devices with their start and end apart: 5 -> 5, of which waited for: 4 -> 2; matrix products, arithmetic and copies ran while one was open for 21% -> 10% of each run, Pallas kernels for 0% -> 0%
where the time goes in v1:
time: 424 us; the launch traced here: 422 us
  blocking collectives  227 us (54%)
  matrix products  61.7 us (15%)
  local copies, waits for them, and re-layouts  44.7 us (11%)
  other arithmetic  36.8 us (9%)
  starting transfers between devices  21.3 us (5%)
  between operations  15.5 us (4%)
  waiting for transfers between devices  15.1 us (4%)
    all_gather x1, blocking collectives, body(): lax.all_gather(mask_rows, 'tm', axis=1, tiled=True)[:, None, None, :] == 1  203 us
    dot_general x1, matrix products, body(): jnp.einsum('sqhc,skhc->shqk', query_heads, key_heads, preferred_element_t...  23.1 us
    reduce_sum x1, other arithmetic, body(): total = jnp.sum(weights, axis=-1)  22.5 us
    dot_general x1, matrix products, body(): jnp.einsum('shqk,skhc->shqc', weights.astype(jnp.bfloat16), value_heads,...  21.9 us
    all_to_all x1, blocking collectives, body(): lax.all_to_all(ctx2, 'probe', split_axis=0, concat_axis=2, tiled=True)  12.4 us
    all_gather x1, blocking collectives, body(): lax.all_gather(slab_mask, 'lane', axis=1, tiled=True)  11.6 us
    another operation x1, local copies, waits for them, and re-layouts  10.4 us
    all_to_all x1, starting transfers between devices, body(): lax.all_to_all(jnp.stack([own_values] * lax.axis_size('tm')), 'tm', 0, 0)  10.2 us
  transfers between devices with their start and end apart: 5, of which 2 were waited for; matrix products, arithmetic and copies ran while one was open for 10% of the time, Pallas kernels for 0%

profile of v1, /device:TPU:1, one launch (start us, length us, event | category | flops | bytes accessed | tf_op | source)
XLA Modules:
  0.0 422.4 jit_solution(9045772824483104259)
XLA Ops:
  8.4 0.7 convert_element_type.146
  9.1 0.7 compare_reduce_fusion.1
  9.8 1.4 multiply_sine_fusion
  11.2 0.8 convolution_reduce_fusion
  12.0 1.0 convolution_reduce_fusion.1
  13.1 1.8 fusion.64
  15.1 0.8 fusion.11
  16.0 0.8 fusion.63
  17.0 3.2 stack.2
  20.2 10.2 %all-to-all-start = ((bf16[16,1,256,768]{2,3,1,0:T(8,128)(2,1)}), bf16[16,1,256,768]{2,3,1,0:T(8,128)(2,1)}, u32[]{:S(2)}, u32[]{:S(2)}) async-start(bf16[16,1,256,768]{2,3,1,0:T(8,128)(2,1)} %stack.2), calls=%async_computation | async-start | bytes 12582912 | tf_op jit(solution)/shard_map/all_to_all | solution.py:83
  30.5 1.8 convolution_convert_fusion.3
  32.4 203.3 %all-gather = bf16[1,1,4096]{2,1,0:T(2,128)(2,1)S(1)} all-gather(bf16[1,1,256]{2,1,0:T(2,128)(2,1)S(1)} %convert_element_type.150), channel_id=2, replica_groups=mesh['probe'=8,'tm'=16,'lane'=2] {'tm'}, dimensions={2}, use_global_device_ids=true | all-gather | bytes 8704 | tf_op jit(solution)/shard_map/all_gather | solution.py:90
  235.8 0.8 fusion.6
  236.6 8.7 %copy.62 = bf16[1,4096,768]{1,2,0:T(8,128)(2,1)} copy(bf16[1,4096,768]{2,1,0:T(8,128)(2,1)} %all-gather.5.cloned.1.call-done) | data formatting | bytes 12582912 | tf_op jit(solution)/shard_map/all_gather | solution.py:78
  245.3 23.1 %select_reduce_fusion = (f32[12,256]{1,0:T(8,128)S(1)}, f32[12,256,4096]{2,1,0:T(8,128)}) fusion(pred[256,4096]{1,0:T(8,128)(4,1)S(1)} %fusion.6, bf16[256,12,64]{0,2,1:T(8,128)(2,1)S(1)} %bitcast.98, bf16[4096,12,64]{0,2,1:T(8,128)(2,1)} %bitcast.92), kind=kOutput, calls=%fused_computation.2 | convolution fusion | flops 1648358400 | bytes 58077184 | tf_op jit(solution)/shard_map/sqhc,skhc->shqk/dot_general | solution.py:86
  268.4 9.0 %copy.64 = bf16[16,1,256,768]{2,0,3,1:T(8,128)(2,1)} copy(bf16[16,1,256,768]{2,3,1,0:T(8,128)(2,1)} %all-to-all-done) | data formatting | bytes 12582912 | tf_op jit(solution)/shard_map/all_to_all | solution.py:83
  277.4 10.4 %reshape.415 = bf16[4096,12,64]{0,2,1:T(8,128)(2,1)} reshape(bf16[16,1,256,768]{2,0,3,1:T(8,128)(2,1)} %copy.64) | data formatting | bytes 12582912 | tf_op jit(solution)/shard_map/reshape.44
  287.8 22.5 %fusion.1 = f32[12,256]{1,0:T(8,128)S(1)} fusion(f32[12,256,4096]{2,1,0:T(8,128)} %get-tuple-element.14, f32[12,256]{1,0:T(8,128)S(1)} %broadcast_maximum_fusion, pred[256,4096]{1,0:T(8,128)(4,1)S(1)} %fusion.6), kind=kLoop, calls=%fused_computation.3 | loop fusion | flops 50328576 | bytes 51404800 | tf_op jit(solution)/shard_map/reduce_sum | solution.py:95
  310.3 21.9 %fusion.43 = bf16[12,256,64]{1,2,0:T(8,128)(2,1)} fusion(bf16[4096,12,64]{0,2,1:T(8,128)(2,1)} %reshape.415, f32[12,256,4096]{2,1,0:T(8,128)} %get-tuple-element.14, f32[12,256]{1,0:T(8,128)S(1)} %broadcast_maximum_fusion, pred[256,4096]{1,0:T(8,128)(4,1)S(1)} %fusion.6, f32[12,256]{1,0:T(8,128)S(1)} %fusion.1), kind=kOutput, calls=%fused_computation.46 | convolution fusion | flops 1661337600 | bytes 58089472 | tf_op jit(solution)/shard_map/shqk,skhc->shqc/dot_general | solution.py:96
  332.2 1.5 fusion.31
  333.7 0.6 copy.82
  334.3 0.5 broadcast.248
  334.8 3.0 reduce.23
  337.8 0.8 reshape.441
  338.7 7.6 %all-to-all-start.2 = ((bf16[8,2,12288]{2,1,0:T(2,128)(2,1)}), bf16[8,2,12288]{2,1,0:T(2,128)(2,1)S(1)}, u32[]{:S(2)}, u32[]{:S(2)}) async-start(bf16[8,2,12288]{2,1,0:T(2,128)(2,1)} %reshape.441), calls=%async_computation.2 | async-start | bytes 786432 | tf_op jit(solution)/shard_map/all_to_all | solution.py:109
  346.4 8.3 %all-to-all-done.2 = bf16[8,2,12288]{2,1,0:T(2,128)(2,1)S(1)} async-done(((bf16[8,2,12288]{2,1,0:T(2,128)(2,1)}), bf16[8,2,12288]{2,1,0:T(2,128)(2,1)S(1)}, u32[]{:S(2)}, u32[]{:S(2)}) %all-to-all-start.2) | async-done | bytes 393248 | tf_op jit(solution)/shard_map/all_to_all | solution.py:109
  354.6 0.4 reshape.442
  355.0 1.2 convert_reduce_fusion
  356.2 3.6 multiply_reduce_fusion
  360.0 3.4 convolution_convert_fusion
  363.4 0.8 copy.65
  364.2 3.4 all-to-all-start.1
  367.9 6.7 %all-to-all-done.1 = bf16[1,1,256]{1,0,2:T(2,128)(2,1)S(1)} async-done(((bf16[1,1,256]{1,0,2:T(2,128)(2,1)}), bf16[1,1,256]{1,0,2:T(2,128)(2,1)S(1)}, u32[]{:S(2)}, u32[]{:S(2)}) %all-to-all-start.1) | async-done | bytes 544 | tf_op jit(solution)/shard_map/all_to_all | solution.py:110
  374.6 1.0 reduce.18
  375.7 11.6 %all_gather.14 = bf16[8,2,32]{2,0,1:T(8,128)(2,1)S(1)} all-gather(bf16[8,1,32]{2,0,1:T(8,128)(2,1)S(1)} %all_to_all.12), channel_id=1, replica_groups=mesh['probe'=8,'tm'=16,'lane'=2] {'lane'}, dimensions={1}, use_global_device_ids=true | all-gather | bytes 1536 | tf_op jit(solution)/shard_map/all_gather | solution.py:125
  387.6 1.8 convolution_convert_fusion.2
  389.4 0.6 reshape.417
  390.0 1.5 copy.69
  391.6 1.3 fusion.62
  392.8 1.4 copy.70
  394.2 2.3 copy.72
  396.6 0.5 fusion.46
  397.1 1.4 fusion.65
  398.5 0.7 fusion.33
  399.2 0.8 copy.73
  400.0 0.6 convert_element_type.174
  400.7 12.4 %all_to_all.35 = bf16[8,1,32,768]{3,2,1,0:T(8,128)(2,1)S(1)} all-to-all(bf16[8,1,32,768]{3,2,1,0:T(8,128)(2,1)S(1)} %bitcast.101), channel_id=1, replica_groups=mesh['probe'=8,'tm'=16,'lane'=2] {'probe'}, dimensions={0} | all-to-all | bytes 786432 | tf_op jit(solution)/shard_map/all_to_all | solution.py:167
  413.1 2.5 fusion.36
  (49 shorter events, 1.7 us)
Async XLA Ops:
  6.5 325.6 %copy-start = (bf16[768,768]{1,0:T(8,128)(2,1)S(1)}, bf16[768,768]{1,0:T(8,128)(2,1)}, u32[]{:S(2)}) copy-start(bf16[768,768]{1,0:T(8,128)(2,1)} %param.24) | copy-start | bytes 3538948
  6.5 8.6 %copy-start.2 = (bf16[768]{0:T(1024)(128)(2,1)S(1)}, bf16[768]{0:T(1024)(128)(2,1)}, u32[]{:S(2)}) copy-start(bf16[768]{0:T(1024)(128)(2,1)} %param.22) | copy-start | bytes 4612
  6.5 230.0 %all-gather.5.cloned.1.call-start = ((), (), s32[]{:S(2)}) async-start(), calls=%async_computation.4 | async-start | bytes 6684672 | tf_op jit(solution)/shard_map/all_gather | solution.py:78
  6.6 8.6 %copy-start.5 = (bf16[768,2304]{1,0:T(8,128)(2,1)S(1)}, bf16[768,2304]{1,0:T(8,128)(2,1)}, u32[]{:S(2)}) copy-start(bf16[768,2304]{1,0:T(8,128)(2,1)} %param.23) | copy-start | bytes 10616836
  20.2 10.2 %copy-start.4 = (s32[1,1,256]{2,1,0:T(1,128)S(1)}, s32[1,1,256]{2,1,0:T(1,128)}, u32[]{:S(2)}) copy-start(s32[1,1,256]{2,1,0:T(1,128)} %param.15) | copy-start | bytes 3076
  20.2 248.2 %all-to-all-start = ((bf16[16,1,256,768]{2,3,1,0:T(8,128)(2,1)}), bf16[16,1,256,768]{2,3,1,0:T(8,128)(2,1)}, u32[]{:S(2)}, u32[]{:S(2)}) async-start(bf16[16,1,256,768]{2,3,1,0:T(8,128)(2,1)} %stack.2), calls=%async_computation | async-start | bytes 12582912 | tf_op jit(solution)/shard_map/all_to_all | solution.py:83
  332.2 14.2 %copy-start.3 = (bf16[768]{0:T(1024)(128)(2,1)S(1)}, bf16[768]{0:T(1024)(128)(2,1)}, u32[]{:S(2)}) copy-start(bf16[768]{0:T(1024)(128)(2,1)} %param.25) | copy-start | bytes 4612
  338.7 16.0 %all-to-all-start.2 = ((bf16[8,2,12288]{2,1,0:T(2,128)(2,1)}), bf16[8,2,12288]{2,1,0:T(2,128)(2,1)S(1)}, u32[]{:S(2)}, u32[]{:S(2)}) async-start(bf16[8,2,12288]{2,1,0:T(2,128)(2,1)} %reshape.441), calls=%async_computation.2 | async-start | bytes 786432 | tf_op jit(solution)/shard_map/all_to_all | solution.py:109
  346.3 43.7 %all-gather.7.cloned.1.call-start = ((), (), s32[]{:S(2)}) async-start(), calls=%async_computation.5 | async-start | bytes 2359296 | tf_op jit(solution)/shard_map/all_gather | solution.py:124
  364.2 10.4 %all-to-all-start.1 = ((bf16[1,1,256]{1,0,2:T(2,128)(2,1)}), bf16[1,1,256]{1,0,2:T(2,128)(2,1)S(1)}, u32[]{:S(2)}, u32[]{:S(2)}) async-start(bf16[1,1,256]{1,0,2:T(2,128)(2,1)} %copy.65), calls=%async_computation.1 | async-start | bytes 262144 | tf_op jit(solution)/shard_map/all_to_all | solution.py:110
  397.1 1.4 copy-start.1
Sparse Core Ops, SparseCore 0:
  16.9 216.7 all-gather.4
  363.5 16.1 all-gather.6
